TPU v7x, 32 devices: a whole 2x2x4 slice. The times are simulated.
32 devices in a mesh: expert: 8 (over y, x, core), tensor: 4 (over z).
Axes of the slice: x: 2, y: 2, z: 4, core: 2. Of those that a mesh axis runs over, the one named last changes fastest.
Arguments:
- tokens: bfloat16 [1024, 7168], P('expert', 'tensor'), may hold values from -6 to 6
- grad_out: bfloat16 [1024, 7168], P('expert', 'tensor'), may hold values from -6 to 6
- expert_ids: int32 [1024, 2], P('expert'), may hold values from 0 to 7, all different within a row; in each aligned block of 128 rows (0 to 127, 128 to 255, ...) at most 64 rows name the same one
- gates: float32 [1024, 2], P('expert'), may hold values from 0.1 to 1
- w_gate: bfloat16 [8, 7168, 2048], P('expert', None, 'tensor'), may hold values from -0.0625 to 0.0625
- w_up: bfloat16 [8, 7168, 2048], P('expert', None, 'tensor'), may hold values from -0.0625 to 0.0625
- w_down: bfloat16 [8, 2048, 7168], P('expert', 'tensor'), may hold values from -0.125 to 0.125
Outputs:
- grad_tokens: bfloat16 [1024, 7168], P('expert', 'tensor')
- grad_w_gate: bfloat16 [8, 7168, 2048], P('expert', None, 'tensor')
- grad_w_up: bfloat16 [8, 7168, 2048], P('expert', None, 'tensor')
- grad_w_down: bfloat16 [8, 2048, 7168], P('expert', 'tensor')
Inputs may be any that keep to these rules, and one draw needn't show every extreme that they name: `expert_ids`: each token names 2 different experts. In each aligned block of 128 tokens (the tokens of one index of the expert axis), no expert is named by more than 64 routes, a bound that some block reaches.
All inputs are finite; a program needn't handle non-finite values.
Results may differ from a plain program's by a relative error of at most 0.0057.
Values may be sent and summed in bfloat16 or wider, within the bound.
No kernel may reach another device: no remote copies, remote signals or barrier semaphores. Data moves between devices by JAX's collectives and lax.ppermute only.
A program may use at most 192 MiB of HBM per device.

v0:
```python
import functools
import math

import jax
import jax.numpy as jnp
from jax import lax
from jax.experimental import pallas as pl
from jax.experimental.pallas import tpu as pltpu
from jax.sharding import PartitionSpec as P

BF16 = jnp.bfloat16
F32 = jnp.float32
LAST = (((1,), (1,)), ((), ()))
FIRST = (((0,), (0,)), ((), ()))
PLAIN = (((1,), (0,)), ((), ()))
FROM = 3
BUNDLE = 48

dot = functools.partial(lax.dot_general, preferred_element_type=F32)


def after(a, *others):
    return lax.optimization_barrier((a,) + others)[0]


def swap(a, mask):
    n = lax.axis_size("expert")
    return lax.ppermute(a, "expert", [(i, i ^ mask) for i in range(n)])


def ring(a):
    n = lax.axis_size("tensor")
    return lax.ppermute(a, "tensor", [(i, (i + 1) % n) for i in range(n)])


class Links:
    def __init__(self, loose=False):
        self.held, self.now, self.loose = [], [], loose

    def turn(self, *work):
        self.held, self.now = self.now + list(work), []

    def send(self, link, a):
        if self.held:
            a = after(a, *self.held)
        out = ring(a) if link == 0 else swap(a, link)
        if not (self.loose and link == 1):
            self.now.append(out)
        return out


def far_masks():
    n = lax.axis_size("expert")
    return [1 << b for b in range(1, n.bit_length() - 1)]


def stack(refs, places, rows):
    return jnp.concatenate([refs[i][at : at + rows, :] for i, at in places], axis=0)


def chunk_of(width, most):
    return max(c for c in range(128, most + 1, 128) if width % c == 0)


def spec(shape, index):
    return pl.BlockSpec(shape, index)


def piece_spec(piece, ck):
    _, rows, block = piece
    return pl.BlockSpec((rows, ck), lambda k, s: (block, k))


def fixed(a):
    return pl.BlockSpec(a.shape, lambda k, s: (0,) * a.ndim)


def kept():
    return pl.BlockSpec(memory_space=pltpu.VMEM)


def call(kernel, name, at, grid, ins, in_specs, outs, out_specs, scratch=(), aliases=None, flops=0):
    moved = sum(math.prod(a.shape) * a.dtype.itemsize for a in [*ins, *outs])
    return pl.pallas_call(
        kernel,
        out_shape=outs,
        grid_spec=pltpu.PrefetchScalarGridSpec(
            num_scalar_prefetch=1,
            grid=(grid,),
            in_specs=in_specs,
            out_specs=out_specs,
            scratch_shapes=list(scratch),
        ),
        input_output_aliases=aliases or {},
        compiler_params=pltpu.CompilerParams(
            dimension_semantics=("arbitrary",), vmem_limit_bytes=48 * 2**20
        ),
        cost_estimate=pl.CostEstimate(flops=flops, bytes_accessed=moved, transcendentals=0),
        name=name,
    )(at, *ins)


def forward(at, parts, rows, weight, wg, wu, wd, sums, final):
    pieces, tok, grd = parts
    arrays = [p[0] for p in pieces]
    n, (width, ff), count = len(arrays), (arrays[0].shape[1], wg.shape[1]), len(tok) * rows
    ck = chunk_of(width, 1792)
    steps = width // ck

    def kernel(_, *refs):
        xs, (w_ref, g_ref, u_ref, d_ref) = refs[:n], refs[n : n + 4]
        before, outs = refs[n + 4 : n + 4 + len(sums)], refs[n + 4 + len(sums) :]
        both, dh = outs[-2:]
        k = pl.program_id(0)

        if final or not sums:

            @pl.when(k == 0)
            def _():
                for i, acc in enumerate((both, dh)):
                    acc[...] = before[i][...] if sums else jnp.zeros_like(acc)

        x = stack(xs, tok, rows)
        both[:, :ff] += dot(x, g_ref[...], PLAIN)
        both[:, ff:] += dot(x, u_ref[...], PLAIN)
        g = (w_ref[...] * stack(xs, grd, rows).astype(F32)).astype(BF16)
        dh[...] += dot(g, d_ref[...], LAST)
        if final:

            @pl.when(k == steps - 1)
            def _():
                for i in range(count // rows):
                    here = slice(i * rows, (i + 1) * rows)
                    gate, upper, down = both[here, :ff], both[here, ff:], dh[here, :]
                    sig = jax.nn.sigmoid(gate)
                    act = gate * sig
                    outs[0][:, here] = (act * upper).T.astype(BF16)
                    slope = upper * sig * (1.0 + gate * (1.0 - sig))
                    outs[1][here, :ff] = (down * slope).astype(BF16)
                    outs[1][here, ff:] = (down * act).astype(BF16)

    accs = [(count, 2 * ff), (count, ff)]
    if final:
        outs = [pltpu.VMEM(s, BF16) for s in ((ff, count), (count, 2 * ff))]
    else:
        outs = [pltpu.VMEM(s, F32) for s in accs]
    in_specs = [piece_spec(p, ck) for p in pieces] + [
        fixed(weight),
        spec((ck, ff), lambda k, s: (s[0] * steps + k, 0)),
        spec((ck, ff), lambda k, s: (s[0] * steps + k, 0)),
        spec((ff, ck), lambda k, s: (0, s[0] * steps + k)),
    ]
    in_specs += [kept()] * len(sums)
    return call(
        kernel, "forward", at, steps, [*arrays, weight, wg, wu, wd, *sums], in_specs,
        outs, [kept() for o in outs],
        scratch=[pltpu.VMEM(s, F32) for s in accs] if final else (),
        aliases={n + 5 + i: i for i in range(len(sums))} if not final else None,
        flops=6 * count * width * ff,
    )


def inputs_back(at, grads, wg, wu, width, upper, got=None):
    count, ff = grads.shape[0], wg.shape[1]
    ck = chunk_of(width, 896)
    steps = width // ck
    half = count // 2

    def kernel(_, a_ref, g_ref, u_ref, *refs):
        part = dot(a_ref[upper * half : (upper + 1) * half, :], jnp.concatenate([g_ref[...], u_ref[...]], axis=1), LAST)
        if got is not None:
            part += refs[0][...].astype(F32)
        refs[-1][...] = part.astype(BF16)

    out = jax.ShapeDtypeStruct((half, width), BF16)
    weights = spec((ck, ff), lambda k, s: (s[0] * steps + k, 0))
    rows = spec((half, ck), lambda k, s: (0, k))
    more = [] if got is None else [got]
    return call(
        kernel, "inputs_back", at, steps, [grads, wg, wu, *more],
        [kept(), weights, weights] + [rows] * len(more),
        [out], [rows],
        flops=4 * half * width * ff,
    )[0]


def weights_back(at, parts, rows, weight, hidden, both, shapes, grads):
    pieces, tok, grd = parts
    arrays = [p[0] for p in pieces]
    n, width, (ff, count) = len(arrays), arrays[0].shape[1], hidden.shape
    ck = chunk_of(width, 896)
    steps = width // ck

    def kernel(_, *refs):
        xs, (w_ref, h_ref, b_ref) = refs[:n], refs[n : n + 3]
        wg_ref, wu_ref, wd_ref = refs[-3:]
        g = (w_ref[...] * stack(xs, grd, rows).astype(F32)).astype(BF16)
        wd_ref[...] = dot(h_ref[...], g, PLAIN).astype(BF16)
        x = stack(xs, tok, rows).T
        wg_ref[...] = dot(x, b_ref[:, :ff], PLAIN).astype(BF16)
        wu_ref[...] = dot(x, b_ref[:, ff:], PLAIN).astype(BF16)

    in_specs = [piece_spec(p, ck) for p in pieces]
    in_specs += [fixed(weight), kept(), kept()]
    in_specs += [pl.BlockSpec(memory_space=pl.ANY)] * len(grads)
    return call(
        kernel, "weights_back", at, steps, [*arrays, weight, hidden, both, *grads], in_specs,
        [jax.ShapeDtypeStruct(s, BF16) for s in shapes],
        [
            spec((ck, ff), lambda k, s: (s[0] * steps + k, 0)),
            spec((ck, ff), lambda k, s: (s[0] * steps + k, 0)),
            spec((ff, ck), lambda k, s: (0, s[0] * steps + k)),
        ],
        aliases={n + 4 + i: i for i in range(len(grads))},
        flops=6 * count * width * ff,
    )


def bundle(own, x, y, rows):
    n, width = own.shape
    ck = chunk_of(width, 896)

    def kernel(own_ref, x_ref, y_ref, to_x_ref, to_y_ref):
        for out, more in ((to_x_ref, y_ref), (to_y_ref, x_ref)):
            out[:n, :] = own_ref[...]
            out[n:, :] = more[...]

    out = jax.ShapeDtypeStruct((n + rows, width), own.dtype)
    whole = spec((n + rows, ck), lambda k: (0, k))
    return pl.pallas_call(
        kernel,
        out_shape=[out, out],
        grid=(width // ck,),
        in_specs=[
            spec((n, ck), lambda k: (0, k)),
            spec((rows, ck), lambda k: (0, k)),
            spec((rows, ck), lambda k: (1, k)),
        ],
        out_specs=[whole, whole],
        compiler_params=pltpu.CompilerParams(vmem_limit_bytes=BUNDLE * 2**20),
        cost_estimate=pl.CostEstimate(flops=0, bytes_accessed=4 * out.size * 2, transcendentals=0),
        name="bundle",
    )(own, x, y)


def onward(mine, xs, ys, later):
    _, rows, width = mine.shape
    h, ck = rows // 2, chunk_of(width, 896)

    def kernel(e_ref, n_ref, x_ref, y_ref, *refs):
        to_x_ref, to_y_ref = refs[-2:]
        to_x_ref[:h, :] = e_ref[0, :h, :]
        to_x_ref[h:rows, :] = (e_ref[0, h:, :].astype(F32) + y_ref[...].astype(F32)).astype(BF16)
        to_y_ref[:h, :] = (n_ref[0, :h, :].astype(F32) + x_ref[...].astype(F32)).astype(BF16)
        to_y_ref[h:rows, :] = n_ref[0, h:, :]
        if later is not None:
            to_x_ref[rows:, :] = refs[0][0, :h, :]
            to_y_ref[rows:, :] = refs[0][0, h:, :]

    more = [] if later is None else [later]
    end = xs.shape[0] // h - 1
    out = jax.ShapeDtypeStruct((rows + h * len(more), width), BF16)
    block = lambda i: spec((1, rows, ck), lambda k: (i, 0, k))
    half = spec((h, ck), lambda k: (end, k))
    whole = spec((out.shape[0], ck), lambda k: (0, k))
    return pl.pallas_call(
        kernel,
        out_shape=[out, out],
        grid=(width // ck,),
        in_specs=[block(1), block(2), half, half] + [block(3)] * len(more),
        out_specs=[whole, whole],
        compiler_params=pltpu.CompilerParams(vmem_limit_bytes=BUNDLE * 2**20),
        cost_estimate=pl.CostEstimate(flops=0, bytes_accessed=8 * out.size, transcendentals=0),
        name="onward",
    )(mine, mine, xs, ys, *more)


def gather_both(links, both, table, use):
    X, Y = far_masks()
    shards = lax.axis_size("tensor")
    rows = both.shape[0] // 2
    hop, xs, ys, near = {0: both}, {}, {}, {}
    tables = [table]
    for r in range(shards + 2):
        work = ()
        if r < shards - 1:
            hop[r + 1] = links.send(0, hop[r])
        if r <= shards:
            if r == 0:
                to_x = to_y = both
            elif r < shards:
                to_x, to_y = bundle(hop[r], xs[r - 1], ys[r - 1], rows)
            else:
                to_x, to_y = ys[r - 1][rows : 2 * rows], xs[r - 1][:rows]
            xs[r] = links.send(X, to_x)
            ys[r] = links.send(Y, to_y)
        if r == 0:
            tables += [links.send(X, table), links.send(Y, table)]
        if r == 1:
            tables.append(links.send(Y, tables[1]))
        if r == 2:
            tables += list(links.send(1, jnp.stack(tables)))
        if 1 <= r <= shards + 1:
            arrays = ([hop[r - 1]] if r <= shards else []) + [xs[r - 1], ys[r - 1]]
            near[r - 1] = [links.send(1, a) for a in arrays]
        if 2 <= r:
            q = r - 2
            block = 2 if q + 1 < shards else 0
            pieces = []
            for here, late in (
                ((hop[q], xs[q], ys[q]), (xs[q + 1], ys[q + 1])),
                (near[q], near[q + 1][-2:]),
            ):
                pieces += [(a, 2 * rows, 0) for a in here] + [(a, rows, block) for a in late]
            tok = [(0, 0), (1, 0), (2, 0), (4, 0), (5, 0), (6, 0), (7, 0), (9, 0)]
            grd = [(0, rows), (1, rows), (2, rows), (3, 0), (5, rows), (6, rows), (7, rows), (8, 0)]
            work = use(q, (pieces, tok, grd), tables)
        links.turn(*work)


def gather_plain(own, table, use):
    rows = own.shape[0] // 2
    tables = [table]
    for m in far_masks() + [1]:
        tables = tables + [swap(t, m) for t in tables]
    for j in range(lax.axis_size("tensor")):
        own = ring(own) if j else own
        pieces = [own]
        for m in far_masks() + [1]:
            pieces = pieces + [swap(p, m) for p in pieces]
        places = range(len(pieces))
        pieces = [(a, 2 * rows, 0) for a in pieces]
        use(j, (pieces, [(i, 0) for i in places], [(i, rows) for i in places]), tables)


def plus(*terms):
    return functools.reduce(lambda a, b: a + b, [t.astype(F32) for t in terms]).astype(BF16)


def on_device(tokens, grad_out, expert_ids, gates, w_gate, w_up, w_down):
    owners, shards = lax.axis_size("expert"), lax.axis_size("tensor")
    me, z = lax.axis_index("expert"), lax.axis_index("tensor")
    rows, width = tokens.shape
    wg, wu, wd = w_gate[0], w_up[0], w_down[0]
    far = far_masks()

    chosen = expert_ids[:, :, None] == jnp.arange(owners, dtype=jnp.int32)
    table = jnp.sum(jnp.where(chosen, gates[:, :, None], 0.0), axis=1).T
    at = [lax.rem(z - j + shards, shards).reshape(1) for j in range(shards)]
    both = jnp.concatenate([tokens, grad_out])
    kept, state = [], {"sums": ()}

    def use(j, parts, tables):
        if j == 0:
            w = [lax.dynamic_index_in_dim(t, me, 0, False) for t in tables]
            state["weight"] = jnp.stack(w).reshape(-1, 1)
        kept.append(parts)
        state["sums"] = forward(
            at[j], parts, rows, state["weight"], wg, wu, wd, state["sums"], j == shards - 1
        )
        return state["sums"]

    links = Links(True)
    if len(far) == 2:
        gather_both(links, both, table, use)
    else:
        gather_plain(both, table, use)
    hidden, dboth = state["sums"]

    order = list(range(1, shards)) + [0]
    grads = ()

    def grads_of(i, *first):
        late = [after(a, *first) for a in (hidden, dboth)]
        return weights_back(
            at[i], kept[i], rows, state["weight"], *late, (wg.shape, wu.shape, wd.shape), grads
        )

    def near_of(j, *first):
        late = after(dboth, *first) if first else dboth
        return inputs_back(at[j], late, wg, wu, width, 1)

    mine_of = lambda j, got: inputs_back(at[j], dboth, wg, wu, width, 0, got).reshape(-1, rows, width)
    if len(far) == 2:
        X, Y = far
        links = Links()
        n, h = shards, rows // 2
        near, got, mine, acc, hop, xs, ys = {0: near_of(order[0])}, {}, {}, {}, {}, {}, {}
        for r in range(1, n + 3):
            last = list(links.held)
            if 4 <= r:
                q = r - 4
                m = mine[q]
                from_x, from_y = xs[q + 3][:rows], ys[q + 3][:rows]
                acc[q] = plus(m[0], from_x, from_y, *([hop[q - 1]] if q else []))
                hop[q] = links.send(0, acc[q])
            if 2 <= r <= n + 1:
                mine[r - 2] = mine_of(order[r - 2], got[r - 2])
            if 3 <= r:
                to_x, to_y = onward(mine[r - 3], xs[r - 1], ys[r - 1], mine.get(r - 2))
            elif r == 2:
                to_x, to_y = mine[0][3, :h], mine[0][3, h:]
            if 2 <= r:
                xs[r] = links.send(X, to_x)
                ys[r] = links.send(Y, to_y)
            if r <= n:
                got[r - 1] = links.send(1, near[r - 1])
            work = []
            if r < n:
                near[r] = near_of(order[r], *last)
                work.append(near[r])
            if r >= FROM and r - FROM < shards:
                grads = grads_of(r - FROM, *last)
                work = work + list(grads)
            links.turn(*work)
        result = plus(mine[n - 1][0], xs[n + 2][:rows], ys[n + 2][:rows], hop[n - 2])
        for i in range(max(0, n + 3 - FROM), shards):
            grads = grads_of(i)
    else:
        result = None
        for j in order:
            mine = mine_of(j, swap(near_of(j), 1))
            for m in reversed(far):
                cut = mine.shape[0] // 2
                mine = plus(mine[:cut], swap(mine[cut:], m))
            terms = [mine[0]] if result is None else [mine[0], ring(result)]
            result = plus(*terms)
        for j in range(shards):
            grads = grads_of(j)
    return (result, grads[0][None], grads[1][None], grads[2][None])


def solution(mesh):
    placed = (
        P("expert", "tensor"),
        P("expert", "tensor"),
        P("expert", None),
        P("expert", None),
        P("expert", None, "tensor"),
        P("expert", None, "tensor"),
        P("expert", "tensor", None),
    )
    return jax.shard_map(
        on_device,
        mesh=mesh,
        in_specs=placed,
        out_specs=(
            P("expert", "tensor"),
            P("expert", None, "tensor"),
            P("expert", None, "tensor"),
            P("expert", "tensor", None),
        ),
        check_vma=False,
    )
```

profile of v0, /device:TPU:0, one launch (start us, length us, event | category | flops | bytes accessed | tf_op | source)
XLA Modules:
  0.0 289.3 jit_solution(14457561676556388209)
XLA Ops:
  2.8 3.1 %collective-permute-start = (bf16[256,1792]{1,0:T(8,128)(2,1)S(1)}, bf16[256,1792]{1,0:T(8,128)(2,1)}, u32[]{:S(2)}, u32[]{:S(2)}) collective-permute-start(bf16[256,1792]{1,0:T(8,128)(2,1)S(1)} %constant_dynamic-update-slice_fusion.refs_0_), channel_id=1, source_target_pairs={{0,1},{1,2},{2,3},{3,0},{4,5},{5,6},{6,7},{7,4},{8,9},{9,10},{10,1... | collective-permute-start | bytes 2752520 | tf_op jit(solution)/shard_map/ppermute | solution.py:33
  10.0 18.3 %collective-permute-done.own_ref.refs_0_ = bf16[256,1792]{1,0:T(8,128)(2,1)} collective-permute-done((bf16[256,1792]{1,0:T(8,128)(2,1)S(1)}, bf16[256,1792]{1,0:T(8,128)(2,1)}, u32[]{:S(2)}, u32[]{:S(2)}) %collective-permute-start) | collective-permute-done | bytes 917536 | tf_op jit(solution)/shard_map/ppermute | solution.py:33
  34.8 28.0 %collective-permute-done.8 = f32[8,128]{1,0:T(8,128)S(1)} collective-permute-done((f32[8,128]{1,0:T(8,128)S(1)}, f32[8,128]{1,0:T(8,128)S(1)}, u32[]{:S(2)}, u32[]{:S(2)}) %collective-permute-start.8) | collective-permute-done | bytes 4128 | tf_op jit(solution)/shard_map/ppermute | solution.py:28
  63.9 2.7 bundle.4
  72.4 10.7 %forward.4 = (f32[1024,1024]{1,0:T(8,128)S(1)}, f32[1024,512]{1,0:T(8,128)S(1)}) custom-call(s32[1]{0:T(128)} %bitcast._, bf16[256,1792]{1,0:T(8,128)(2,1)} %copy-done.33, bf16[256,1792]{1,0:T(8,128)(2,1)} %copy-done.27, bf16[256,1792]{1,0:T(8,128)(2,1)} %collective-permute-done.2.y_ref.refs_2_, ...), custom_call_target="tpu_custom_call" | custom-call | flops 5637144576 | bytes 39325696 | tf_op jit(solution)/shard_map/forward/pallas_call | solution.py:84
  86.4 8.6 %collective-permute-done.9.own_ref.refs_0_ = bf16[256,1792]{1,0:T(8,128)(2,1)} collective-permute-done((bf16[256,1792]{1,0:T(8,128)(2,1)}, bf16[256,1792]{1,0:T(8,128)(2,1)}, u32[]{:S(2)}, u32[]{:S(2)}) %collective-permute-start.9) | collective-permute-done | bytes 917536 | tf_op jit(solution)/shard_map/ppermute | solution.py:33
  95.1 4.0 %collective-permute-done.10.x_ref.refs_3_.refs_1_ = bf16[384,1792]{1,0:T(8,128)(2,1)S(1)} collective-permute-done((bf16[384,1792]{1,0:T(8,128)(2,1)}, bf16[384,1792]{1,0:T(8,128)(2,1)S(1)}, u32[]{:S(2)}, u32[]{:S(2)}) %collective-permute-start.10) | collective-permute-done | bytes 1376288 | tf_op jit(solution)/shard_map/ppermute | solution.py:28
  100.7 2.9 %bundle.5 = (bf16[384,1792]{1,0:T(8,128)(2,1)}, bf16[384,1792]{1,0:T(8,128)(2,1)}) custom-call(bf16[256,1792]{1,0:T(8,128)(2,1)} %collective-permute-done.9.own_ref.refs_0_, bf16[384,1792]{1,0:T(8,128)(2,1)S(1)} %collective-permute-done.10.x_ref.refs_3_.refs_1_, bf16[384,1792]{1,0:T(8,128)(2,1)} %copy-done.10), custom_call_target="tpu_custom_call" | custom-call | bytes 5505024 | tf_op jit(solution)/shard_map/bundle/pallas_call | solution.py:230
  110.3 10.8 %forward.5 = (f32[1024,1024]{1,0:T(8,128)S(1)}, f32[1024,512]{1,0:T(8,128)S(1)}) custom-call(s32[1]{0:T(128)} %bitcast.16._, bf16[256,1792]{1,0:T(8,128)(2,1)} %collective-permute-done.own_ref.refs_0_, bf16[384,1792]{1,0:T(8,128)(2,1)} %collective-permute-done.6.x_ref.refs_3_.refs_1_, ...), custom_call_target="tpu_custom_call", output_to_operand_aliasing={{0}: (15, {}), {1}: (16, {})} | custom-call | flops 5637144576 | bytes 47452160 | tf_op jit(solution)/shard_map/forward/pallas_call | solution.py:84
  124.4 11.6 %collective-permute-done.18.refs_3_.refs_1_ = bf16[384,1792]{1,0:T(8,128)(2,1)} collective-permute-done((bf16[384,1792]{1,0:T(8,128)(2,1)}, bf16[384,1792]{1,0:T(8,128)(2,1)}, u32[]{:S(2)}, u32[]{:S(2)}) %collective-permute-start.18) | collective-permute-done | bytes 1376288 | tf_op jit(solution)/shard_map/ppermute | solution.py:28
  147.5 10.8 %forward.6 = (f32[1024,1024]{1,0:T(8,128)S(1)}, f32[1024,512]{1,0:T(8,128)S(1)}) custom-call(s32[1]{0:T(128)} %bitcast.17._, bf16[256,1792]{1,0:T(8,128)(2,1)} %copy-done.24, bf16[384,1792]{1,0:T(8,128)(2,1)} %copy-done.8, bf16[384,1792]{1,0:T(8,128)(2,1)} %copy-done.10, ...), custom_call_target="tpu_custom_call", output_to_operand_aliasing={{0}: (15, {}), {1}: (16, {})} | custom-call | flops 5637144576 | bytes 47452160 | tf_op jit(solution)/shard_map/forward/pallas_call | solution.py:84
  164.1 12.6 %forward.7 = (bf16[512,1024]{1,0:T(8,128)(2,1)S(1)}, bf16[1024,1024]{1,0:T(8,128)(2,1)S(1)}) custom-call(s32[1]{0:T(128)} %bitcast.1._, bf16[256,1792]{1,0:T(8,128)(2,1)} %collective-permute-done.9.own_ref.refs_0_, bf16[384,1792]{1,0:T(8,128)(2,1)} %collective-permute-done.18.refs_3_.refs_1_, bf16[384,1792]{1,0:T(8,128)(2,1)} %collective-permute-done.19.refs_4_.refs_2_, ...), custom_call_target="tpu_custom_call" | custom-call | flops 5637144576 | bytes 40636416 | tf_op jit(solution)/shard_map/forward/pallas_call | solution.py:84
  177.7 4.9 %inputs_back.8 = bf16[512,1792]{1,0:T(8,128)(2,1)S(1)} custom-call(s32[1]{0:T(128)} %bitcast.16._, bf16[1024,1024]{1,0:T(8,128)(2,1)S(1)} %get-tuple-element.170.a_ref.refs_12_, bf16[7168,512]{1,0:T(8,128)(2,1)} %bitcast.51, bf16[7168,512]{1,0:T(8,128)(2,1)} %bitcast.63), custom_call_target="tpu_custom_call" | custom-call | flops 1879048192 | bytes 18612224 | tf_op jit(solution)/shard_map/inputs_back/pallas_call | solution.py:84
  182.9 4.2 %inputs_back.10 = bf16[512,1792]{1,0:T(8,128)(2,1)S(1)} custom-call(s32[1]{0:T(128)} %bitcast.17._, bf16[1024,1024]{1,0:T(8,128)(2,1)S(1)} %get-tuple-element.170.a_ref.refs_12_, bf16[7168,512]{1,0:T(8,128)(2,1)} %bitcast.52, bf16[7168,512]{1,0:T(8,128)(2,1)} %bitcast.64), custom_call_target="tpu_custom_call" | custom-call | flops 1879048192 | bytes 18612224 | tf_op jit(solution)/shard_map/inputs_back/pallas_call | solution.py:84
  187.5 4.2 %inputs_back.9 = bf16[512,1792]{1,0:T(8,128)(2,1)S(1)} custom-call(s32[1]{0:T(128)} %bitcast.16._, bf16[1024,1024]{1,0:T(8,128)(2,1)S(1)} %get-tuple-element.170.a_ref.refs_12_, bf16[7168,512]{1,0:T(8,128)(2,1)} %bitcast.53, bf16[7168,512]{1,0:T(8,128)(2,1)} %bitcast.65, bf16[512,1792]{1,0:T(8,128)(2,1)S(1)} %collective-permute-done.31.refs_0_), custom_call_target="tpu_custom_call" | custom-call | flops 1879048192 | bytes 20447232 | tf_op jit(solution)/shard_map/inputs_back/pallas_call | solution.py:84
  193.9 5.1 %inputs_back.11 = bf16[512,1792]{1,0:T(8,128)(2,1)} custom-call(s32[1]{0:T(128)} %bitcast.1._, bf16[1024,1024]{1,0:T(8,128)(2,1)S(1)} %get-tuple-element.170.a_ref.refs_12_, bf16[7168,512]{1,0:T(8,128)(2,1)} %bitcast.54, bf16[7168,512]{1,0:T(8,128)(2,1)} %bitcast.66), custom_call_target="tpu_custom_call" | custom-call | flops 1879048192 | bytes 18612224 | tf_op jit(solution)/shard_map/inputs_back/pallas_call | solution.py:84
  200.0 4.2 %inputs_back.13 = bf16[512,1792]{1,0:T(8,128)(2,1)S(1)} custom-call(s32[1]{0:T(128)} %bitcast.17._, bf16[1024,1024]{1,0:T(8,128)(2,1)S(1)} %get-tuple-element.170.a_ref.refs_12_, bf16[7168,512]{1,0:T(8,128)(2,1)} %bitcast.55, bf16[7168,512]{1,0:T(8,128)(2,1)} %bitcast.67, bf16[512,1792]{1,0:T(8,128)(2,1)S(1)} %collective-permute-done.34.refs_0_), custom_call_target="tpu_custom_call" | custom-call | flops 1879048192 | bytes 20447232 | tf_op jit(solution)/shard_map/inputs_back/pallas_call | solution.py:84
  208.4 4.3 %inputs_back.12 = bf16[512,1792]{1,0:T(8,128)(2,1)S(1)} custom-call(s32[1]{0:T(128)} %bitcast._, bf16[1024,1024]{1,0:T(8,128)(2,1)S(1)} %get-tuple-element.170.a_ref.refs_12_, bf16[7168,512]{1,0:T(8,128)(2,1)} %bitcast.56, bf16[7168,512]{1,0:T(8,128)(2,1)} %bitcast.68), custom_call_target="tpu_custom_call" | custom-call | flops 1879048192 | bytes 18612224 | tf_op jit(solution)/shard_map/inputs_back/pallas_call | solution.py:84
  214.0 11.3 %weights_back.4 = (bf16[7168,512]{1,0:T(8,128)(2,1)}, bf16[7168,512]{1,0:T(8,128)(2,1)}, bf16[512,7168]{1,0:T(8,128)(2,1)}) custom-call(s32[1]{0:T(128)} %bitcast._, bf16[256,1792]{1,0:T(8,128)(2,1)S(1)} %copy-done.34, bf16[256,1792]{1,0:T(8,128)(2,1)S(1)} %copy-done.28, bf16[256,1792]{1,0:T(8,128)(2,1)} %collective-permute-done.2.y_ref.refs_2_, ...), custom_call_target="tpu_custom_call" | custom-call | flops 5637144576 | bytes 36179968 | tf_op jit(solution)/shard_map/weights_back/pallas_call | solution.py:84
  226.4 4.7 %inputs_back.15 = bf16[512,1792]{1,0:T(8,128)(2,1)S(1)} custom-call(s32[1]{0:T(128)} %bitcast.1._, bf16[1024,1024]{1,0:T(8,128)(2,1)S(1)} %copy-done.1, bf16[7168,512]{1,0:T(8,128)(2,1)} %bitcast.57, bf16[7168,512]{1,0:T(8,128)(2,1)} %bitcast.69, bf16[512,1792]{1,0:T(8,128)(2,1)} %collective-permute-done.37.refs_0_), custom_call_target="tpu_custom_call" | custom-call | flops 1879048192 | bytes 20447232 | tf_op jit(solution)/shard_map/inputs_back/pallas_call | solution.py:84
  236.3 11.3 %weights_back.5 = (bf16[7168,512]{1,0:T(8,128)(2,1)}, bf16[7168,512]{1,0:T(8,128)(2,1)}, bf16[512,7168]{1,0:T(8,128)(2,1)}) custom-call(s32[1]{0:T(128)} %bitcast.16._, bf16[256,1792]{1,0:T(8,128)(2,1)} %collective-permute-done.own_ref.refs_0_, ...), custom_call_target="tpu_custom_call", output_to_operand_aliasing={{0}: (14, {}), {1}: (15, {}), {2}: (16, {})} | custom-call | flops 5637144576 | bytes 60035072 | tf_op jit(solution)/shard_map/weights_back/pallas_call | solution.py:84
  247.6 4.6 %inputs_back.14 = bf16[512,1792]{1,0:T(8,128)(2,1)S(1)} custom-call(s32[1]{0:T(128)} %bitcast._, bf16[1024,1024]{1,0:T(8,128)(2,1)S(1)} %copy-done.2, bf16[7168,512]{1,0:T(8,128)(2,1)} %bitcast.58, bf16[7168,512]{1,0:T(8,128)(2,1)} %bitcast.70, bf16[512,1792]{1,0:T(8,128)(2,1)} %collective-permute-done.38.refs_0_), custom_call_target="tpu_custom_call" | custom-call | flops 1879048192 | bytes 20447232 | tf_op jit(solution)/shard_map/inputs_back/pallas_call | solution.py:84
  261.0 10.2 %weights_back.6 = (bf16[7168,512]{1,0:T(8,128)(2,1)}, bf16[7168,512]{1,0:T(8,128)(2,1)}, bf16[512,7168]{1,0:T(8,128)(2,1)}) custom-call(s32[1]{0:T(128)} %bitcast.17._, bf16[256,1792]{1,0:T(8,128)(2,1)S(1)} %copy-done.26, bf16[384,1792]{1,0:T(8,128)(2,1)S(1)} %copy-done.9, ...), custom_call_target="tpu_custom_call", output_to_operand_aliasing={{0}: (14, {}), {1}: (15, {}), {2}: (16, {})} | custom-call | flops 5637144576 | bytes 60035072 | tf_op jit(solution)/shard_map/weights_back/pallas_call | solution.py:84
  277.6 10.2 %weights_back.7 = (bf16[7168,512]{1,0:T(8,128)(2,1)}, bf16[7168,512]{1,0:T(8,128)(2,1)}, bf16[512,7168]{1,0:T(8,128)(2,1)}) custom-call(s32[1]{0:T(128)} %bitcast.1._, bf16[256,1792]{1,0:T(8,128)(2,1)} %collective-permute-done.9.own_ref.refs_0_, ...), custom_call_target="tpu_custom_call", output_to_operand_aliasing={{0}: (14, {}), {1}: (15, {}), {2}: (16, {})} | custom-call | flops 5637144576 | bytes 56365056 | tf_op jit(solution)/shard_map/weights_back/pallas_call | solution.py:84
  (191 shorter events, 84.1 us)
Async XLA Ops:
  2.8 25.6 %collective-permute-start = (bf16[256,1792]{1,0:T(8,128)(2,1)S(1)}, bf16[256,1792]{1,0:T(8,128)(2,1)}, u32[]{:S(2)}, u32[]{:S(2)}) collective-permute-start(bf16[256,1792]{1,0:T(8,128)(2,1)S(1)} %constant_dynamic-update-slice_fusion.refs_0_), channel_id=1, source_target_pairs={{0,1},{1,2},{2,3},{3,0},{4,5},{5,6},{6,7},{7,4},{8,9},{9,10},{10,1... | collective-permute-start | bytes 2752520 | tf_op jit(solution)/shard_map/ppermute | solution.py:33
  5.9 22.5 %collective-permute-start.1 = (bf16[256,1792]{1,0:T(8,128)(2,1)S(1)}, bf16[256,1792]{1,0:T(8,128)(2,1)S(1)}, u32[]{:S(2)}, u32[]{:S(2)}) collective-permute-start(bf16[256,1792]{1,0:T(8,128)(2,1)S(1)} %constant_dynamic-update-slice_fusion.refs_0_), channel_id=1, source_target_pairs={{0,8},{4,12},{8,0},{12,4},{16,24},{20,28},{24,16},{28,20},{1,9},{5... | collective-permute-start | bytes 2752520 | tf_op jit(solution)/shard_map/ppermute | solution.py:28
  7.3 21.7 %collective-permute-start.2 = (bf16[256,1792]{1,0:T(8,128)(2,1)S(1)}, bf16[256,1792]{1,0:T(8,128)(2,1)}, u32[]{:S(2)}, u32[]{:S(2)}) collective-permute-start(bf16[256,1792]{1,0:T(8,128)(2,1)S(1)} %constant_dynamic-update-slice_fusion.refs_0_), channel_id=1, source_target_pairs={{0,16},{4,20},{8,24},{12,28},{16,0},{20,4},{24,8},{28,12},{1,17},{... | collective-permute-start | bytes 2752520 | tf_op jit(solution)/shard_map/ppermute | solution.py:28
  8.9 21.7 %collective-permute-start.3 = (f32[8,128]{1,0:T(8,128)S(1)}, f32[8,128]{1,0:T(8,128)S(1)}, u32[]{:S(2)}, u32[]{:S(2)}) collective-permute-start(f32[8,128]{1,0:T(8,128)S(1)} %bitcast.79), channel_id=1, source_target_pairs={{0,8},{4,12},{8,0},{12,4},{16,24},{20,28},{24,16},{28,20},{1,9},{5... | collective-permute-start | bytes 12296 | tf_op jit(solution)/shard_map/ppermute | solution.py:28
  9.5 21.1 %collective-permute-start.4 = (f32[8,128]{1,0:T(8,128)S(1)}, f32[8,128]{1,0:T(8,128)S(1)}, u32[]{:S(2)}, u32[]{:S(2)}) collective-permute-start(f32[8,128]{1,0:T(8,128)S(1)} %bitcast.80), channel_id=1, source_target_pairs={{0,16},{4,20},{8,24},{12,28},{16,0},{20,4},{24,8},{28,12},{1,17},{... | collective-permute-start | bytes 12296 | tf_op jit(solution)/shard_map/ppermute | solution.py:28
  30.6 32.7 %collective-permute-start.6 = (bf16[384,1792]{1,0:T(8,128)(2,1)S(1)}, bf16[384,1792]{1,0:T(8,128)(2,1)}, u32[]{:S(2)}, u32[]{:S(2)}) collective-permute-start(bf16[384,1792]{1,0:T(8,128)(2,1)S(1)} %get-tuple-element.91), channel_id=1, source_target_pairs={{0,8},{4,12},{8,0},{12,4},{16,24},{20,28},{24,16},{28,20},{1,9},{5... | collective-permute-start | bytes 4128776 | tf_op jit(solution)/shard_map/ppermute | solution.py:28
  31.8 31.5 %collective-permute-start.7 = (bf16[384,1792]{1,0:T(8,128)(2,1)S(1)}, bf16[384,1792]{1,0:T(8,128)(2,1)}, u32[]{:S(2)}, u32[]{:S(2)}) collective-permute-start(bf16[384,1792]{1,0:T(8,128)(2,1)S(1)} %get-tuple-element.93), channel_id=1, source_target_pairs={{0,16},{4,20},{8,24},{12,28},{16,0},{20,4},{24,8},{28,12},{1,17},{... | collective-permute-start | bytes 4128776 | tf_op jit(solution)/shard_map/ppermute | solution.py:28
  33.3 29.5 %collective-permute-start.5 = (bf16[256,1792]{1,0:T(8,128)(2,1)}, bf16[256,1792]{1,0:T(8,128)(2,1)S(1)}, u32[]{:S(2)}, u32[]{:S(2)}) collective-permute-start(bf16[256,1792]{1,0:T(8,128)(2,1)} %collective-permute-done.own_ref.refs_0_), channel_id=1, source_target_pairs={{0,1},{1,2},{2,3},{3,0},{4,5},{5,6},{6,7},{7,4},{8,9},{9,10},{10,1... | collective-permute-start | bytes 2752520 | tf_op jit(solution)/shard_map/ppermute | solution.py:33
  34.3 28.5 %collective-permute-start.8 = (f32[8,128]{1,0:T(8,128)S(1)}, f32[8,128]{1,0:T(8,128)S(1)}, u32[]{:S(2)}, u32[]{:S(2)}) collective-permute-start(f32[8,128]{1,0:T(8,128)S(1)} %collective-permute-done.3), channel_id=1, source_target_pairs={{0,16},{4,20},{8,24},{12,28},{16,0},{20,4},{24,8},{28,12},{1,17},{... | collective-permute-start | bytes 12296 | tf_op jit(solution)/shard_map/ppermute | solution.py:28
  34.8 31.8 %collective-permute-start.12 = (bf16[256,1792]{1,0:T(8,128)(2,1)S(1)}, bf16[256,1792]{1,0:T(8,128)(2,1)}, u32[]{:S(2)}, u32[]{:S(2)}) collective-permute-start(bf16[256,1792]{1,0:T(8,128)(2,1)S(1)} %constant_dynamic-update-slice_fusion.refs_0_), channel_id=1, source_target_pairs={{0,4},{4,0},{8,12},{12,8},{16,20},{20,16},{24,28},{28,24},{1,5},{5... | collective-permute-start | bytes 2752520 | tf_op jit(solution)/shard_map/ppermute | solution.py:28
  66.6 32.5 %collective-permute-start.10 = (bf16[384,1792]{1,0:T(8,128)(2,1)}, bf16[384,1792]{1,0:T(8,128)(2,1)S(1)}, u32[]{:S(2)}, u32[]{:S(2)}) collective-permute-start(bf16[384,1792]{1,0:T(8,128)(2,1)} %get-tuple-element.97), channel_id=1, source_target_pairs={{0,8},{4,12},{8,0},{12,4},{16,24},{20,28},{24,16},{28,20},{1,9},{5... | collective-permute-start | bytes 4128776 | tf_op jit(solution)/shard_map/ppermute | solution.py:28
  67.5 32.1 %collective-permute-start.11 = (bf16[384,1792]{1,0:T(8,128)(2,1)}, bf16[384,1792]{1,0:T(8,128)(2,1)S(1)}, u32[]{:S(2)}, u32[]{:S(2)}) collective-permute-start(bf16[384,1792]{1,0:T(8,128)(2,1)} %get-tuple-element.99), channel_id=1, source_target_pairs={{0,16},{4,20},{8,24},{12,28},{16,0},{20,4},{24,8},{28,12},{1,17},{... | collective-permute-start | bytes 4128776 | tf_op jit(solution)/shard_map/ppermute | solution.py:28
  70.6 24.5 %collective-permute-start.9 = (bf16[256,1792]{1,0:T(8,128)(2,1)}, bf16[256,1792]{1,0:T(8,128)(2,1)}, u32[]{:S(2)}, u32[]{:S(2)}) collective-permute-start(bf16[256,1792]{1,0:T(8,128)(2,1)} %copy-done.24), channel_id=1, source_target_pairs={{0,1},{1,2},{2,3},{3,0},{4,5},{5,6},{6,7},{7,4},{8,9},{9,10},{10,1... | collective-permute-start | bytes 2752520 | tf_op jit(solution)/shard_map/ppermute | solution.py:33
  103.7 32.4 %collective-permute-start.18 = (bf16[384,1792]{1,0:T(8,128)(2,1)}, bf16[384,1792]{1,0:T(8,128)(2,1)}, u32[]{:S(2)}, u32[]{:S(2)}) collective-permute-start(bf16[384,1792]{1,0:T(8,128)(2,1)} %get-tuple-element.109), channel_id=1, source_target_pairs={{0,8},{4,12},{8,0},{12,4},{16,24},{20,28},{24,16},{28,20},{1,9},{5... | collective-permute-start | bytes 4128776 | tf_op jit(solution)/shard_map/ppermute | solution.py:28
  105.0 32.0 %collective-permute-start.19 = (bf16[384,1792]{1,0:T(8,128)(2,1)}, bf16[384,1792]{1,0:T(8,128)(2,1)}, u32[]{:S(2)}, u32[]{:S(2)}) collective-permute-start(bf16[384,1792]{1,0:T(8,128)(2,1)} %get-tuple-element.111), channel_id=1, source_target_pairs={{0,16},{4,20},{8,24},{12,28},{16,0},{20,4},{24,8},{28,12},{1,17},{... | collective-permute-start | bytes 4128776 | tf_op jit(solution)/shard_map/ppermute | solution.py:28
  138.6 23.1 %collective-permute-start.23 = (bf16[128,1792]{1,0:T(8,128)(2,1)S(1)}, bf16[128,1792]{1,0:T(8,128)(2,1)S(1)}, u32[]{:S(2)}, u32[]{:S(2)}) collective-permute-start(bf16[128,1792]{1,0:T(8,128)(2,1)S(1)} %slice.60), channel_id=1, source_target_pairs={{0,8},{4,12},{8,0},{12,4},{16,24},{20,28},{24,16},{28,20},{1,9},{5... | collective-permute-start | bytes 1376264 | tf_op jit(solution)/shard_map/ppermute | solution.py:28
  140.5 21.2 %collective-permute-start.24 = (bf16[128,1792]{1,0:T(8,128)(2,1)S(1)}, bf16[128,1792]{1,0:T(8,128)(2,1)S(1)}, u32[]{:S(2)}, u32[]{:S(2)}) collective-permute-start(bf16[128,1792]{1,0:T(8,128)(2,1)S(1)} %slice.61), channel_id=1, source_target_pairs={{0,16},{4,20},{8,24},{12,28},{16,0},{20,4},{24,8},{28,12},{1,17},{... | collective-permute-start | bytes 1376264 | tf_op jit(solution)/shard_map/ppermute | solution.py:28
  142.8 19.4 %collective-permute-start.25 = (bf16[256,1792]{1,0:T(8,128)(2,1)}, bf16[256,1792]{1,0:T(8,128)(2,1)S(1)}, u32[]{:S(2)}, u32[]{:S(2)}) collective-permute-start(bf16[256,1792]{1,0:T(8,128)(2,1)} %collective-permute-done.9.own_ref.refs_0_), channel_id=1, source_target_pairs={{0,4},{4,0},{8,12},{12,8},{16,20},{20,16},{24,28},{28,24},{1,5},{5... | collective-permute-start | bytes 2752520 | tf_op jit(solution)/shard_map/ppermute | solution.py:28
  200.0 25.3 %collective-permute-start.37 = (bf16[512,1792]{1,0:T(8,128)(2,1)}, bf16[512,1792]{1,0:T(8,128)(2,1)}, u32[]{:S(2)}, u32[]{:S(2)}) collective-permute-start(bf16[512,1792]{1,0:T(8,128)(2,1)} %inputs_back.11), channel_id=1, source_target_pairs={{0,4},{4,0},{8,12},{12,8},{16,20},{20,16},{24,28},{28,24},{1,5},{5... | collective-permute-start | bytes 5505032 | tf_op jit(solution)/shard_map/ppermute | solution.py:28
  205.6 19.7 %collective-permute-start.36 = (bf16[192,1792]{1,0:T(8,128)(2,1)}, bf16[192,1792]{1,0:T(8,128)(2,1)S(1)}, u32[]{:S(2)}, u32[]{:S(2)}) collective-permute-start(bf16[192,1792]{1,0:T(8,128)(2,1)} %get-tuple-element.136), channel_id=1, source_target_pairs={{0,16},{4,20},{8,24},{12,28},{16,0},{20,4},{24,8},{28,12},{1,17},{... | collective-permute-start | bytes 2064392 | tf_op jit(solution)/shard_map/ppermute | solution.py:28
  206.9 18.4 %collective-permute-start.35 = (bf16[192,1792]{1,0:T(8,128)(2,1)}, bf16[192,1792]{1,0:T(8,128)(2,1)S(1)}, u32[]{:S(2)}, u32[]{:S(2)}) collective-permute-start(bf16[192,1792]{1,0:T(8,128)(2,1)} %get-tuple-element.134), channel_id=1, source_target_pairs={{0,8},{4,12},{8,0},{12,4},{16,24},{20,28},{24,16},{28,20},{1,9},{5... | collective-permute-start | bytes 2064392 | tf_op jit(solution)/shard_map/ppermute | solution.py:28
  225.3 22.3 %collective-permute-start.38 = (bf16[512,1792]{1,0:T(8,128)(2,1)}, bf16[512,1792]{1,0:T(8,128)(2,1)}, u32[]{:S(2)}, u32[]{:S(2)}) collective-permute-start(bf16[512,1792]{1,0:T(8,128)(2,1)} %copy-done.35), channel_id=1, source_target_pairs={{0,4},{4,0},{8,12},{12,8},{16,20},{20,16},{24,28},{28,24},{1,5},{5... | collective-permute-start | bytes 5505032 | tf_op jit(solution)/shard_map/ppermute | solution.py:28
  225.6 30.1 %collective-permute-start.41 = (bf16[128,1792]{1,0:T(8,128)(2,1)S(1)}, bf16[128,1792]{1,0:T(8,128)(2,1)}, u32[]{:S(2)}, u32[]{:S(2)}) collective-permute-start(bf16[128,1792]{1,0:T(8,128)(2,1)S(1)} %add_convert_fusion.3), channel_id=1, source_target_pairs={{0,1},{1,2},{2,3},{3,0},{4,5},{5,6},{6,7},{7,4},{8,9},{9,10},{10,1... | collective-permute-start | bytes 1376264 | tf_op jit(solution)/shard_map/ppermute | solution.py:33
  234.6 18.9 %collective-permute-start.40 = (bf16[192,1792]{1,0:T(8,128)(2,1)}, bf16[192,1792]{1,0:T(8,128)(2,1)S(1)}, u32[]{:S(2)}, u32[]{:S(2)}) collective-permute-start(bf16[192,1792]{1,0:T(8,128)(2,1)} %get-tuple-element.147), channel_id=1, source_target_pairs={{0,16},{4,20},{8,24},{12,28},{16,0},{20,4},{24,8},{28,12},{1,17},{... | collective-permute-start | bytes 2064392 | tf_op jit(solution)/shard_map/ppermute | solution.py:28
  (62 other events, 513.9 us)
where the time goes:
time: 295 us; the launch traced here: 289 us
  Pallas kernels  138 us (47%)
  waiting for transfers between devices  82.2 us (28%)
  starting transfers between devices  37 us (13%)
  local copies, waits for them, and re-layouts  28.3 us (10%)
    pallas_call x16, Pallas kernels, call(): pl.pallas_call(kernel, out_shape=outs, grid_spec=pltpu.PrefetchScalarGrid...  124 us
    ppermute x42, waiting for transfers between devices, swap(): return lax.ppermute(a, 'expert', [(i, i ^ mask) for i in range(n)])  53.5 us
    ppermute x6, waiting for transfers between devices, ring(): return lax.ppermute(a, 'tensor', [(i, (i + 1) % n) for i in range(n)])  28.6 us
    ppermute x42, starting transfers between devices, swap(): return lax.ppermute(a, 'expert', [(i, i ^ mask) for i in range(n)])  28.5 us
    unnamed x77, local copies, waits for them, and re-layouts  24 us
    ppermute x6, starting transfers between devices, ring(): return lax.ppermute(a, 'tensor', [(i, (i + 1) % n) for i in range(n)])  8.49 us
    pallas_call x3, Pallas kernels, bundle(): pl.pallas_call(kernel, out_shape=[out, out], grid=(width // ck,), in_spec...  7.24 us
    pallas_call x4, Pallas kernels, onward(): pl.pallas_call(kernel, out_shape=[out, out], grid=(width // ck,), in_spec...  6.14 us
  transfers between devices with their start and end apart: 48, of which 18 were waited for; matrix products, arithmetic and copies ran while one was open for 2% of the time, Pallas kernels for 41%

commit v1 on v0

--- a/solution.py
+++ b/solution.py
@@ -383,7 +383,7 @@
     mine_of = lambda j, got: inputs_back(at[j], dboth, wg, wu, width, 0, got).reshape(-1, rows, width)
     if len(far) == 2:
         X, Y = far
-        links = Links()
+        links = Links(True)
         n, h = shards, rows // 2
         near, got, mine, acc, hop, xs, ys = {0: near_of(order[0])}, {}, {}, {}, {}, {}, {}
         for r in range(1, n + 3):

time: 295 us -> 294 us (level)
  transfers between devices with their start and end apart: 48 -> 48, of which waited for: 18 -> 17; matrix products, arithmetic and copies ran while one was open for 2% -> 2% of each run, Pallas kernels for 41% -> 41%
where the time goes in v1:
time: 294 us; the launch traced here: 288 us
  Pallas kernels  138 us (47%)
  waiting for transfers between devices  81.9 us (28%)
  starting transfers between devices  36.5 us (12%)
  local copies, waits for them, and re-layouts  28.2 us (10%)
    pallas_call x16, Pallas kernels, call(): pl.pallas_call(kernel, out_shape=outs, grid_spec=pltpu.PrefetchScalarGrid...  124 us
    ppermute x42, waiting for transfers between devices, swap(): return lax.ppermute(a, 'expert', [(i, i ^ mask) for i in range(n)])  53.2 us
    ppermute x6, waiting for transfers between devices, ring(): return lax.ppermute(a, 'tensor', [(i, (i + 1) % n) for i in range(n)])  28.7 us
    ppermute x42, starting transfers between devices, swap(): return lax.ppermute(a, 'expert', [(i, i ^ mask) for i in range(n)])  28 us
    unnamed x77, local copies, waits for them, and re-layouts  23.9 us
    ppermute x6, starting transfers between devices, ring(): return lax.ppermute(a, 'tensor', [(i, (i + 1) % n) for i in range(n)])  8.46 us
    pallas_call x3, Pallas kernels, bundle(): pl.pallas_call(kernel, out_shape=[out, out], grid=(width // ck,), in_spec...  7.24 us
    pallas_call x4, Pallas kernels, onward(): pl.pallas_call(kernel, out_shape=[out, out], grid=(width // ck,), in_spec...  6.11 us
  transfers between devices with their start and end apart: 48, of which 17 were waited for; matrix products, arithmetic and copies ran while one was open for 2% of the time, Pallas kernels for 41%

profile of v1, /device:TPU:0, one launch (start us, length us, event | category | flops | bytes accessed | tf_op | source)
XLA Modules:
  0.0 288.4 jit_solution(12688151297435071247)
XLA Ops:
  2.8 3.1 %collective-permute-start = (bf16[256,1792]{1,0:T(8,128)(2,1)S(1)}, bf16[256,1792]{1,0:T(8,128)(2,1)}, u32[]{:S(2)}, u32[]{:S(2)}) collective-permute-start(bf16[256,1792]{1,0:T(8,128)(2,1)S(1)} %constant_dynamic-update-slice_fusion.refs_0_), channel_id=1, source_target_pairs={{0,1},{1,2},{2,3},{3,0},{4,5},{5,6},{6,7},{7,4},{8,9},{9,10},{10,1... | collective-permute-start | bytes 2752520 | tf_op jit(solution)/shard_map/ppermute | solution.py:33
  10.0 18.3 %collective-permute-done.own_ref.refs_0_ = bf16[256,1792]{1,0:T(8,128)(2,1)} collective-permute-done((bf16[256,1792]{1,0:T(8,128)(2,1)S(1)}, bf16[256,1792]{1,0:T(8,128)(2,1)}, u32[]{:S(2)}, u32[]{:S(2)}) %collective-permute-start) | collective-permute-done | bytes 917536 | tf_op jit(solution)/shard_map/ppermute | solution.py:33
  34.8 28.0 %collective-permute-done.8 = f32[8,128]{1,0:T(8,128)S(1)} collective-permute-done((f32[8,128]{1,0:T(8,128)S(1)}, f32[8,128]{1,0:T(8,128)S(1)}, u32[]{:S(2)}, u32[]{:S(2)}) %collective-permute-start.8) | collective-permute-done | bytes 4128 | tf_op jit(solution)/shard_map/ppermute | solution.py:28
  63.9 2.8 bundle.4
  72.4 10.7 %forward.4 = (f32[1024,1024]{1,0:T(8,128)S(1)}, f32[1024,512]{1,0:T(8,128)S(1)}) custom-call(s32[1]{0:T(128)} %bitcast._, bf16[256,1792]{1,0:T(8,128)(2,1)} %copy-done.33, bf16[256,1792]{1,0:T(8,128)(2,1)} %copy-done.27, bf16[256,1792]{1,0:T(8,128)(2,1)} %collective-permute-done.2.y_ref.refs_2_, ...), custom_call_target="tpu_custom_call" | custom-call | flops 5637144576 | bytes 39325696 | tf_op jit(solution)/shard_map/forward/pallas_call | solution.py:84
  86.4 8.7 %collective-permute-done.9.own_ref.refs_0_ = bf16[256,1792]{1,0:T(8,128)(2,1)} collective-permute-done((bf16[256,1792]{1,0:T(8,128)(2,1)}, bf16[256,1792]{1,0:T(8,128)(2,1)}, u32[]{:S(2)}, u32[]{:S(2)}) %collective-permute-start.9) | collective-permute-done | bytes 917536 | tf_op jit(solution)/shard_map/ppermute | solution.py:33
  95.1 4.0 %collective-permute-done.10.x_ref.refs_3_.refs_1_ = bf16[384,1792]{1,0:T(8,128)(2,1)S(1)} collective-permute-done((bf16[384,1792]{1,0:T(8,128)(2,1)}, bf16[384,1792]{1,0:T(8,128)(2,1)S(1)}, u32[]{:S(2)}, u32[]{:S(2)}) %collective-permute-start.10) | collective-permute-done | bytes 1376288 | tf_op jit(solution)/shard_map/ppermute | solution.py:28
  100.7 2.9 %bundle.5 = (bf16[384,1792]{1,0:T(8,128)(2,1)}, bf16[384,1792]{1,0:T(8,128)(2,1)}) custom-call(bf16[256,1792]{1,0:T(8,128)(2,1)} %collective-permute-done.9.own_ref.refs_0_, bf16[384,1792]{1,0:T(8,128)(2,1)S(1)} %collective-permute-done.10.x_ref.refs_3_.refs_1_, bf16[384,1792]{1,0:T(8,128)(2,1)} %copy-done.10), custom_call_target="tpu_custom_call" | custom-call | bytes 5505024 | tf_op jit(solution)/shard_map/bundle/pallas_call | solution.py:230
  110.3 10.8 %forward.5 = (f32[1024,1024]{1,0:T(8,128)S(1)}, f32[1024,512]{1,0:T(8,128)S(1)}) custom-call(s32[1]{0:T(128)} %bitcast.16._, bf16[256,1792]{1,0:T(8,128)(2,1)} %collective-permute-done.own_ref.refs_0_, bf16[384,1792]{1,0:T(8,128)(2,1)} %collective-permute-done.6.x_ref.refs_3_.refs_1_, ...), custom_call_target="tpu_custom_call", output_to_operand_aliasing={{0}: (15, {}), {1}: (16, {})} | custom-call | flops 5637144576 | bytes 47452160 | tf_op jit(solution)/shard_map/forward/pallas_call | solution.py:84
  124.4 11.7 %collective-permute-done.18.refs_3_.refs_1_ = bf16[384,1792]{1,0:T(8,128)(2,1)} collective-permute-done((bf16[384,1792]{1,0:T(8,128)(2,1)}, bf16[384,1792]{1,0:T(8,128)(2,1)}, u32[]{:S(2)}, u32[]{:S(2)}) %collective-permute-start.18) | collective-permute-done | bytes 1376288 | tf_op jit(solution)/shard_map/ppermute | solution.py:28
  147.5 10.8 %forward.6 = (f32[1024,1024]{1,0:T(8,128)S(1)}, f32[1024,512]{1,0:T(8,128)S(1)}) custom-call(s32[1]{0:T(128)} %bitcast.17._, bf16[256,1792]{1,0:T(8,128)(2,1)} %copy-done.24, bf16[384,1792]{1,0:T(8,128)(2,1)} %copy-done.8, bf16[384,1792]{1,0:T(8,128)(2,1)} %copy-done.10, ...), custom_call_target="tpu_custom_call", output_to_operand_aliasing={{0}: (15, {}), {1}: (16, {})} | custom-call | flops 5637144576 | bytes 47452160 | tf_op jit(solution)/shard_map/forward/pallas_call | solution.py:84
  164.1 12.6 %forward.7 = (bf16[512,1024]{1,0:T(8,128)(2,1)S(1)}, bf16[1024,1024]{1,0:T(8,128)(2,1)S(1)}) custom-call(s32[1]{0:T(128)} %bitcast.1._, bf16[256,1792]{1,0:T(8,128)(2,1)} %collective-permute-done.9.own_ref.refs_0_, bf16[384,1792]{1,0:T(8,128)(2,1)} %collective-permute-done.18.refs_3_.refs_1_, bf16[384,1792]{1,0:T(8,128)(2,1)} %collective-permute-done.19.refs_4_.refs_2_, ...), custom_call_target="tpu_custom_call" | custom-call | flops 5637144576 | bytes 40636416 | tf_op jit(solution)/shard_map/forward/pallas_call | solution.py:84
  177.7 4.9 %inputs_back.8 = bf16[512,1792]{1,0:T(8,128)(2,1)S(1)} custom-call(s32[1]{0:T(128)} %bitcast.16._, bf16[1024,1024]{1,0:T(8,128)(2,1)S(1)} %get-tuple-element.170.a_ref.refs_12_, bf16[7168,512]{1,0:T(8,128)(2,1)} %bitcast.51, bf16[7168,512]{1,0:T(8,128)(2,1)} %bitcast.63), custom_call_target="tpu_custom_call" | custom-call | flops 1879048192 | bytes 18612224 | tf_op jit(solution)/shard_map/inputs_back/pallas_call | solution.py:84
  182.9 4.2 %inputs_back.10 = bf16[512,1792]{1,0:T(8,128)(2,1)S(1)} custom-call(s32[1]{0:T(128)} %bitcast.17._, bf16[1024,1024]{1,0:T(8,128)(2,1)S(1)} %get-tuple-element.170.a_ref.refs_12_, bf16[7168,512]{1,0:T(8,128)(2,1)} %bitcast.52, bf16[7168,512]{1,0:T(8,128)(2,1)} %bitcast.64), custom_call_target="tpu_custom_call" | custom-call | flops 1879048192 | bytes 18612224 | tf_op jit(solution)/shard_map/inputs_back/pallas_call | solution.py:84
  187.5 4.2 %inputs_back.9 = bf16[512,1792]{1,0:T(8,128)(2,1)S(1)} custom-call(s32[1]{0:T(128)} %bitcast.16._, bf16[1024,1024]{1,0:T(8,128)(2,1)S(1)} %get-tuple-element.170.a_ref.refs_12_, bf16[7168,512]{1,0:T(8,128)(2,1)} %bitcast.53, bf16[7168,512]{1,0:T(8,128)(2,1)} %bitcast.65, bf16[512,1792]{1,0:T(8,128)(2,1)S(1)} %collective-permute-done.31.refs_0_), custom_call_target="tpu_custom_call" | custom-call | flops 1879048192 | bytes 20447232 | tf_op jit(solution)/shard_map/inputs_back/pallas_call | solution.py:84
  193.9 5.0 %inputs_back.11 = bf16[512,1792]{1,0:T(8,128)(2,1)} custom-call(s32[1]{0:T(128)} %bitcast.1._, bf16[1024,1024]{1,0:T(8,128)(2,1)S(1)} %get-tuple-element.170.a_ref.refs_12_, bf16[7168,512]{1,0:T(8,128)(2,1)} %bitcast.54, bf16[7168,512]{1,0:T(8,128)(2,1)} %bitcast.66), custom_call_target="tpu_custom_call" | custom-call | flops 1879048192 | bytes 18612224 | tf_op jit(solution)/shard_map/inputs_back/pallas_call | solution.py:84
  198.9 4.2 %inputs_back.13 = bf16[512,1792]{1,0:T(8,128)(2,1)S(1)} custom-call(s32[1]{0:T(128)} %bitcast.17._, bf16[1024,1024]{1,0:T(8,128)(2,1)S(1)} %get-tuple-element.170.a_ref.refs_12_, bf16[7168,512]{1,0:T(8,128)(2,1)} %bitcast.55, bf16[7168,512]{1,0:T(8,128)(2,1)} %bitcast.67, bf16[512,1792]{1,0:T(8,128)(2,1)S(1)} %collective-permute-done.34.refs_0_), custom_call_target="tpu_custom_call" | custom-call | flops 1879048192 | bytes 20447232 | tf_op jit(solution)/shard_map/inputs_back/pallas_call | solution.py:84
  206.5 4.3 %inputs_back.12 = bf16[512,1792]{1,0:T(8,128)(2,1)S(1)} custom-call(s32[1]{0:T(128)} %bitcast._, bf16[1024,1024]{1,0:T(8,128)(2,1)S(1)} %get-tuple-element.170.a_ref.refs_12_, bf16[7168,512]{1,0:T(8,128)(2,1)} %bitcast.56, bf16[7168,512]{1,0:T(8,128)(2,1)} %bitcast.68), custom_call_target="tpu_custom_call" | custom-call | flops 1879048192 | bytes 18612224 | tf_op jit(solution)/shard_map/inputs_back/pallas_call | solution.py:84
  212.1 11.3 %weights_back.4 = (bf16[7168,512]{1,0:T(8,128)(2,1)}, bf16[7168,512]{1,0:T(8,128)(2,1)}, bf16[512,7168]{1,0:T(8,128)(2,1)}) custom-call(s32[1]{0:T(128)} %bitcast._, bf16[256,1792]{1,0:T(8,128)(2,1)S(1)} %copy-done.34, bf16[256,1792]{1,0:T(8,128)(2,1)S(1)} %copy-done.28, bf16[256,1792]{1,0:T(8,128)(2,1)} %collective-permute-done.2.y_ref.refs_2_, ...), custom_call_target="tpu_custom_call" | custom-call | flops 5637144576 | bytes 36179968 | tf_op jit(solution)/shard_map/weights_back/pallas_call | solution.py:84
  225.1 4.8 %inputs_back.15 = bf16[512,1792]{1,0:T(8,128)(2,1)S(1)} custom-call(s32[1]{0:T(128)} %bitcast.1._, bf16[1024,1024]{1,0:T(8,128)(2,1)S(1)} %copy-done.1, bf16[7168,512]{1,0:T(8,128)(2,1)} %bitcast.57, bf16[7168,512]{1,0:T(8,128)(2,1)} %bitcast.69, bf16[512,1792]{1,0:T(8,128)(2,1)} %collective-permute-done.38.refs_0_), custom_call_target="tpu_custom_call" | custom-call | flops 1879048192 | bytes 20447232 | tf_op jit(solution)/shard_map/inputs_back/pallas_call | solution.py:84
  235.7 11.4 %weights_back.5 = (bf16[7168,512]{1,0:T(8,128)(2,1)}, bf16[7168,512]{1,0:T(8,128)(2,1)}, bf16[512,7168]{1,0:T(8,128)(2,1)}) custom-call(s32[1]{0:T(128)} %bitcast.16._, bf16[256,1792]{1,0:T(8,128)(2,1)} %collective-permute-done.own_ref.refs_0_, ...), custom_call_target="tpu_custom_call", output_to_operand_aliasing={{0}: (14, {}), {1}: (15, {}), {2}: (16, {})} | custom-call | flops 5637144576 | bytes 60035072 | tf_op jit(solution)/shard_map/weights_back/pallas_call | solution.py:84
  247.1 4.6 %inputs_back.14 = bf16[512,1792]{1,0:T(8,128)(2,1)S(1)} custom-call(s32[1]{0:T(128)} %bitcast._, bf16[1024,1024]{1,0:T(8,128)(2,1)S(1)} %copy-done.2, bf16[7168,512]{1,0:T(8,128)(2,1)} %bitcast.58, bf16[7168,512]{1,0:T(8,128)(2,1)} %bitcast.70, bf16[512,1792]{1,0:T(8,128)(2,1)} %collective-permute-done.37.refs_0_), custom_call_target="tpu_custom_call" | custom-call | flops 1879048192 | bytes 20447232 | tf_op jit(solution)/shard_map/inputs_back/pallas_call | solution.py:84
  259.7 10.2 %weights_back.6 = (bf16[7168,512]{1,0:T(8,128)(2,1)}, bf16[7168,512]{1,0:T(8,128)(2,1)}, bf16[512,7168]{1,0:T(8,128)(2,1)}) custom-call(s32[1]{0:T(128)} %bitcast.17._, bf16[256,1792]{1,0:T(8,128)(2,1)S(1)} %copy-done.26, bf16[384,1792]{1,0:T(8,128)(2,1)S(1)} %copy-done.9, ...), custom_call_target="tpu_custom_call", output_to_operand_aliasing={{0}: (14, {}), {1}: (15, {}), {2}: (16, {})} | custom-call | flops 5637144576 | bytes 60035072 | tf_op jit(solution)/shard_map/weights_back/pallas_call | solution.py:84
  276.8 10.2 %weights_back.7 = (bf16[7168,512]{1,0:T(8,128)(2,1)}, bf16[7168,512]{1,0:T(8,128)(2,1)}, bf16[512,7168]{1,0:T(8,128)(2,1)}) custom-call(s32[1]{0:T(128)} %bitcast.1._, bf16[256,1792]{1,0:T(8,128)(2,1)} %collective-permute-done.9.own_ref.refs_0_, ...), custom_call_target="tpu_custom_call", output_to_operand_aliasing={{0}: (14, {}), {1}: (15, {}), {2}: (16, {})} | custom-call | flops 5637144576 | bytes 56365056 | tf_op jit(solution)/shard_map/weights_back/pallas_call | solution.py:84
  (191 shorter events, 83.2 us)
Async XLA Ops:
  2.8 25.6 %collective-permute-start = (bf16[256,1792]{1,0:T(8,128)(2,1)S(1)}, bf16[256,1792]{1,0:T(8,128)(2,1)}, u32[]{:S(2)}, u32[]{:S(2)}) collective-permute-start(bf16[256,1792]{1,0:T(8,128)(2,1)S(1)} %constant_dynamic-update-slice_fusion.refs_0_), channel_id=1, source_target_pairs={{0,1},{1,2},{2,3},{3,0},{4,5},{5,6},{6,7},{7,4},{8,9},{9,10},{10,1... | collective-permute-start | bytes 2752520 | tf_op jit(solution)/shard_map/ppermute | solution.py:33
  5.9 22.5 %collective-permute-start.1 = (bf16[256,1792]{1,0:T(8,128)(2,1)S(1)}, bf16[256,1792]{1,0:T(8,128)(2,1)S(1)}, u32[]{:S(2)}, u32[]{:S(2)}) collective-permute-start(bf16[256,1792]{1,0:T(8,128)(2,1)S(1)} %constant_dynamic-update-slice_fusion.refs_0_), channel_id=1, source_target_pairs={{0,8},{4,12},{8,0},{12,4},{16,24},{20,28},{24,16},{28,20},{1,9},{5... | collective-permute-start | bytes 2752520 | tf_op jit(solution)/shard_map/ppermute | solution.py:28
  7.3 21.7 %collective-permute-start.2 = (bf16[256,1792]{1,0:T(8,128)(2,1)S(1)}, bf16[256,1792]{1,0:T(8,128)(2,1)}, u32[]{:S(2)}, u32[]{:S(2)}) collective-permute-start(bf16[256,1792]{1,0:T(8,128)(2,1)S(1)} %constant_dynamic-update-slice_fusion.refs_0_), channel_id=1, source_target_pairs={{0,16},{4,20},{8,24},{12,28},{16,0},{20,4},{24,8},{28,12},{1,17},{... | collective-permute-start | bytes 2752520 | tf_op jit(solution)/shard_map/ppermute | solution.py:28
  8.9 21.7 %collective-permute-start.3 = (f32[8,128]{1,0:T(8,128)S(1)}, f32[8,128]{1,0:T(8,128)S(1)}, u32[]{:S(2)}, u32[]{:S(2)}) collective-permute-start(f32[8,128]{1,0:T(8,128)S(1)} %bitcast.79), channel_id=1, source_target_pairs={{0,8},{4,12},{8,0},{12,4},{16,24},{20,28},{24,16},{28,20},{1,9},{5... | collective-permute-start | bytes 12296 | tf_op jit(solution)/shard_map/ppermute | solution.py:28
  9.5 21.1 %collective-permute-start.4 = (f32[8,128]{1,0:T(8,128)S(1)}, f32[8,128]{1,0:T(8,128)S(1)}, u32[]{:S(2)}, u32[]{:S(2)}) collective-permute-start(f32[8,128]{1,0:T(8,128)S(1)} %bitcast.80), channel_id=1, source_target_pairs={{0,16},{4,20},{8,24},{12,28},{16,0},{20,4},{24,8},{28,12},{1,17},{... | collective-permute-start | bytes 12296 | tf_op jit(solution)/shard_map/ppermute | solution.py:28
  30.6 32.7 %collective-permute-start.6 = (bf16[384,1792]{1,0:T(8,128)(2,1)S(1)}, bf16[384,1792]{1,0:T(8,128)(2,1)}, u32[]{:S(2)}, u32[]{:S(2)}) collective-permute-start(bf16[384,1792]{1,0:T(8,128)(2,1)S(1)} %get-tuple-element.91), channel_id=1, source_target_pairs={{0,8},{4,12},{8,0},{12,4},{16,24},{20,28},{24,16},{28,20},{1,9},{5... | collective-permute-start | bytes 4128776 | tf_op jit(solution)/shard_map/ppermute | solution.py:28
  31.8 31.5 %collective-permute-start.7 = (bf16[384,1792]{1,0:T(8,128)(2,1)S(1)}, bf16[384,1792]{1,0:T(8,128)(2,1)}, u32[]{:S(2)}, u32[]{:S(2)}) collective-permute-start(bf16[384,1792]{1,0:T(8,128)(2,1)S(1)} %get-tuple-element.93), channel_id=1, source_target_pairs={{0,16},{4,20},{8,24},{12,28},{16,0},{20,4},{24,8},{28,12},{1,17},{... | collective-permute-start | bytes 4128776 | tf_op jit(solution)/shard_map/ppermute | solution.py:28
  33.3 29.5 %collective-permute-start.5 = (bf16[256,1792]{1,0:T(8,128)(2,1)}, bf16[256,1792]{1,0:T(8,128)(2,1)S(1)}, u32[]{:S(2)}, u32[]{:S(2)}) collective-permute-start(bf16[256,1792]{1,0:T(8,128)(2,1)} %collective-permute-done.own_ref.refs_0_), channel_id=1, source_target_pairs={{0,1},{1,2},{2,3},{3,0},{4,5},{5,6},{6,7},{7,4},{8,9},{9,10},{10,1... | collective-permute-start | bytes 2752520 | tf_op jit(solution)/shard_map/ppermute | solution.py:33
  34.3 28.5 %collective-permute-start.8 = (f32[8,128]{1,0:T(8,128)S(1)}, f32[8,128]{1,0:T(8,128)S(1)}, u32[]{:S(2)}, u32[]{:S(2)}) collective-permute-start(f32[8,128]{1,0:T(8,128)S(1)} %collective-permute-done.3), channel_id=1, source_target_pairs={{0,16},{4,20},{8,24},{12,28},{16,0},{20,4},{24,8},{28,12},{1,17},{... | collective-permute-start | bytes 12296 | tf_op jit(solution)/shard_map/ppermute | solution.py:28
  34.8 31.8 %collective-permute-start.12 = (bf16[256,1792]{1,0:T(8,128)(2,1)S(1)}, bf16[256,1792]{1,0:T(8,128)(2,1)}, u32[]{:S(2)}, u32[]{:S(2)}) collective-permute-start(bf16[256,1792]{1,0:T(8,128)(2,1)S(1)} %constant_dynamic-update-slice_fusion.refs_0_), channel_id=1, source_target_pairs={{0,4},{4,0},{8,12},{12,8},{16,20},{20,16},{24,28},{28,24},{1,5},{5... | collective-permute-start | bytes 2752520 | tf_op jit(solution)/shard_map/ppermute | solution.py:28
  66.7 32.5 %collective-permute-start.10 = (bf16[384,1792]{1,0:T(8,128)(2,1)}, bf16[384,1792]{1,0:T(8,128)(2,1)S(1)}, u32[]{:S(2)}, u32[]{:S(2)}) collective-permute-start(bf16[384,1792]{1,0:T(8,128)(2,1)} %get-tuple-element.97), channel_id=1, source_target_pairs={{0,8},{4,12},{8,0},{12,4},{16,24},{20,28},{24,16},{28,20},{1,9},{5... | collective-permute-start | bytes 4128776 | tf_op jit(solution)/shard_map/ppermute | solution.py:28
  67.5 32.1 %collective-permute-start.11 = (bf16[384,1792]{1,0:T(8,128)(2,1)}, bf16[384,1792]{1,0:T(8,128)(2,1)S(1)}, u32[]{:S(2)}, u32[]{:S(2)}) collective-permute-start(bf16[384,1792]{1,0:T(8,128)(2,1)} %get-tuple-element.99), channel_id=1, source_target_pairs={{0,16},{4,20},{8,24},{12,28},{16,0},{20,4},{24,8},{28,12},{1,17},{... | collective-permute-start | bytes 4128776 | tf_op jit(solution)/shard_map/ppermute | solution.py:28
  70.6 24.5 %collective-permute-start.9 = (bf16[256,1792]{1,0:T(8,128)(2,1)}, bf16[256,1792]{1,0:T(8,128)(2,1)}, u32[]{:S(2)}, u32[]{:S(2)}) collective-permute-start(bf16[256,1792]{1,0:T(8,128)(2,1)} %copy-done.24), channel_id=1, source_target_pairs={{0,1},{1,2},{2,3},{3,0},{4,5},{5,6},{6,7},{7,4},{8,9},{9,10},{10,1... | collective-permute-start | bytes 2752520 | tf_op jit(solution)/shard_map/ppermute | solution.py:33
  103.6 32.4 %collective-permute-start.18 = (bf16[384,1792]{1,0:T(8,128)(2,1)}, bf16[384,1792]{1,0:T(8,128)(2,1)}, u32[]{:S(2)}, u32[]{:S(2)}) collective-permute-start(bf16[384,1792]{1,0:T(8,128)(2,1)} %get-tuple-element.109), channel_id=1, source_target_pairs={{0,8},{4,12},{8,0},{12,4},{16,24},{20,28},{24,16},{28,20},{1,9},{5... | collective-permute-start | bytes 4128776 | tf_op jit(solution)/shard_map/ppermute | solution.py:28
  104.9 32.1 %collective-permute-start.19 = (bf16[384,1792]{1,0:T(8,128)(2,1)}, bf16[384,1792]{1,0:T(8,128)(2,1)}, u32[]{:S(2)}, u32[]{:S(2)}) collective-permute-start(bf16[384,1792]{1,0:T(8,128)(2,1)} %get-tuple-element.111), channel_id=1, source_target_pairs={{0,16},{4,20},{8,24},{12,28},{16,0},{20,4},{24,8},{28,12},{1,17},{... | collective-permute-start | bytes 4128776 | tf_op jit(solution)/shard_map/ppermute | solution.py:28
  138.6 23.1 %collective-permute-start.23 = (bf16[128,1792]{1,0:T(8,128)(2,1)S(1)}, bf16[128,1792]{1,0:T(8,128)(2,1)S(1)}, u32[]{:S(2)}, u32[]{:S(2)}) collective-permute-start(bf16[128,1792]{1,0:T(8,128)(2,1)S(1)} %slice.60), channel_id=1, source_target_pairs={{0,8},{4,12},{8,0},{12,4},{16,24},{20,28},{24,16},{28,20},{1,9},{5... | collective-permute-start | bytes 1376264 | tf_op jit(solution)/shard_map/ppermute | solution.py:28
  140.5 21.2 %collective-permute-start.24 = (bf16[128,1792]{1,0:T(8,128)(2,1)S(1)}, bf16[128,1792]{1,0:T(8,128)(2,1)S(1)}, u32[]{:S(2)}, u32[]{:S(2)}) collective-permute-start(bf16[128,1792]{1,0:T(8,128)(2,1)S(1)} %slice.61), channel_id=1, source_target_pairs={{0,16},{4,20},{8,24},{12,28},{16,0},{20,4},{24,8},{28,12},{1,17},{... | collective-permute-start | bytes 1376264 | tf_op jit(solution)/shard_map/ppermute | solution.py:28
  142.8 19.4 %collective-permute-start.25 = (bf16[256,1792]{1,0:T(8,128)(2,1)}, bf16[256,1792]{1,0:T(8,128)(2,1)S(1)}, u32[]{:S(2)}, u32[]{:S(2)}) collective-permute-start(bf16[256,1792]{1,0:T(8,128)(2,1)} %collective-permute-done.9.own_ref.refs_0_), channel_id=1, source_target_pairs={{0,4},{4,0},{8,12},{12,8},{16,20},{20,16},{24,28},{28,24},{1,5},{5... | collective-permute-start | bytes 2752520 | tf_op jit(solution)/shard_map/ppermute | solution.py:28
  204.5 18.9 %collective-permute-start.35 = (bf16[192,1792]{1,0:T(8,128)(2,1)}, bf16[192,1792]{1,0:T(8,128)(2,1)S(1)}, u32[]{:S(2)}, u32[]{:S(2)}) collective-permute-start(bf16[192,1792]{1,0:T(8,128)(2,1)} %get-tuple-element.134), channel_id=1, source_target_pairs={{0,8},{4,12},{8,0},{12,4},{16,24},{20,28},{24,16},{28,20},{1,9},{5... | collective-permute-start | bytes 2064392 | tf_op jit(solution)/shard_map/ppermute | solution.py:28
  206.0 19.1 %collective-permute-start.38 = (bf16[512,1792]{1,0:T(8,128)(2,1)}, bf16[512,1792]{1,0:T(8,128)(2,1)}, u32[]{:S(2)}, u32[]{:S(2)}) collective-permute-start(bf16[512,1792]{1,0:T(8,128)(2,1)} %inputs_back.11), channel_id=1, source_target_pairs={{0,4},{4,0},{8,12},{12,8},{16,20},{20,16},{24,28},{28,24},{1,5},{5... | collective-permute-start | bytes 5505032 | tf_op jit(solution)/shard_map/ppermute | solution.py:28
  224.1 23.0 %collective-permute-start.37 = (bf16[512,1792]{1,0:T(8,128)(2,1)}, bf16[512,1792]{1,0:T(8,128)(2,1)}, u32[]{:S(2)}, u32[]{:S(2)}) collective-permute-start(bf16[512,1792]{1,0:T(8,128)(2,1)} %copy-done.35), channel_id=1, source_target_pairs={{0,4},{4,0},{8,12},{12,8},{16,20},{20,16},{24,28},{28,24},{1,5},{5... | collective-permute-start | bytes 5505032 | tf_op jit(solution)/shard_map/ppermute | solution.py:28
  224.3 30.9 %collective-permute-start.41 = (bf16[128,1792]{1,0:T(8,128)(2,1)S(1)}, bf16[128,1792]{1,0:T(8,128)(2,1)}, u32[]{:S(2)}, u32[]{:S(2)}) collective-permute-start(bf16[128,1792]{1,0:T(8,128)(2,1)S(1)} %add_convert_fusion.3), channel_id=1, source_target_pairs={{0,1},{1,2},{2,3},{3,0},{4,5},{5,6},{6,7},{7,4},{8,9},{9,10},{10,1... | collective-permute-start | bytes 1376264 | tf_op jit(solution)/shard_map/ppermute | solution.py:33
  233.4 19.6 %collective-permute-start.40 = (bf16[192,1792]{1,0:T(8,128)(2,1)}, bf16[192,1792]{1,0:T(8,128)(2,1)S(1)}, u32[]{:S(2)}, u32[]{:S(2)}) collective-permute-start(bf16[192,1792]{1,0:T(8,128)(2,1)} %get-tuple-element.147), channel_id=1, source_target_pairs={{0,16},{4,20},{8,24},{12,28},{16,0},{20,4},{24,8},{28,12},{1,17},{... | collective-permute-start | bytes 2064392 | tf_op jit(solution)/shard_map/ppermute | solution.py:28
  234.6 18.5 %collective-permute-start.39 = (bf16[192,1792]{1,0:T(8,128)(2,1)}, bf16[192,1792]{1,0:T(8,128)(2,1)S(1)}, u32[]{:S(2)}, u32[]{:S(2)}) collective-permute-start(bf16[192,1792]{1,0:T(8,128)(2,1)} %get-tuple-element.145), channel_id=1, source_target_pairs={{0,8},{4,12},{8,0},{12,4},{16,24},{20,28},{24,16},{28,20},{1,9},{5... | collective-permute-start | bytes 2064392 | tf_op jit(solution)/shard_map/ppermute | solution.py:28
  (62 other events, 517.0 us)
